TPU v7x, 32 devices: a whole 2x2x4 slice. The times are simulated.
32 devices in a mesh: row: 8 (over y, x, core), col: 4 (over z).
Axes of the slice: x: 2, y: 2, z: 4, core: 2. Of those that a mesh axis runs over, the one named last changes fastest.
Arguments:
- orbitals: float32 [16384, 1024], P('row', 'col'), may hold values from -6 to 6
- point_index: int32 [8192], replicated, may hold values from 0 to 16383, as said below
- coulomb: float32 [8192, 8192], P('row', 'col'), may hold values from -0.001953125 to 0.001953125
- fitting: float32 [16384, 8192], P('row', 'col'), may hold values from -0.0625 to 0.0625
Outputs:
- exchange_out: float32 [16384, 1024], P('row', 'col')
Inputs may be any that keep to these rules, and one draw needn't show every extreme that they name: `point_index`: indices are distinct. Grid index g lies in slab g // 2048. Of the 1024 consecutive points of each row panel, at most 256 lie in one slab, and in every panel exactly 256 lie in one slab.
All inputs are finite; a program needn't handle non-finite values.
Results may differ from a plain program's by a relative error of at most 0.00012.
Values sent between devices are 32-bit elements; how exact they have to be, the bound alone decides.
A program may use at most 128 MiB of HBM per device.

v0:
```python
import jax
import jax.numpy as jnp
from jax import lax
from jax.sharding import PartitionSpec as P


def broadcast(x, axis, root):
    mine = lax.axis_index(axis) == root
    return lax.psum(jnp.where(mine, x, jnp.zeros_like(x)), axis)


def per_device(orbitals, point_index, coulomb, fitting):
    row_count = lax.axis_size("row")
    col_count = lax.axis_size("col")
    ratio = row_count // col_count
    slab_rows = orbitals.shape[0]
    band_cols = orbitals.shape[1]
    total_points = point_index.shape[0]
    per_panel = total_points // row_count
    slot_count = 2 * per_panel // row_count
    my_row = lax.axis_index("row")
    my_col = lax.axis_index("col")
    owner = point_index // slab_rows
    local_row = point_index - owner * slab_rows
    owner_grid = owner.reshape(row_count, per_panel)
    local_grid = local_row.reshape(row_count, per_panel)
    matches = (owner_grid[:, :, None] == jnp.arange(row_count)[None, None, :]).astype(jnp.int32)
    ranking = jnp.cumsum(matches, axis=1) - 1
    slot_grid = jnp.sum(jnp.where(matches > 0, ranking, 0), axis=2)
    mine = owner_grid == my_row
    chosen = mine[:, :, None] & (slot_grid[:, :, None] == jnp.arange(slot_count)[None, None, :])
    source_row = jnp.sum(jnp.where(chosen, local_grid[:, :, None], 0), axis=1)
    valid = jnp.any(chosen, axis=1)
    outgoing = jnp.where(valid[:, :, None], orbitals[source_row], 0.0)
    received = lax.all_to_all(outgoing, "row", split_axis=0, concat_axis=0, tiled=True)
    flattened = received.reshape(row_count * slot_count, band_cols)
    owner_mine = lax.dynamic_slice_in_dim(owner_grid, my_row, 1, 0)[0]
    slot_mine = lax.dynamic_slice_in_dim(slot_grid, my_row, 1, 0)[0]
    panel_strip = flattened[owner_mine * slot_count + slot_mine]
    panel_full = lax.all_gather(panel_strip, "col", axis=1, tiled=True)
    picked_parts = []
    for offset in range(ratio):
        picked_parts.append(broadcast(panel_full, "row", my_col * ratio + offset))
    column_full = jnp.concatenate(picked_parts, axis=0)
    pair = jnp.dot(
        panel_full,
        column_full.T,
        precision=lax.Precision.HIGHEST,
        preferred_element_type=jnp.float32,
    )
    partial_value = jnp.dot(
        coulomb * pair,
        column_full,
        precision=lax.Precision.HIGHEST,
        preferred_element_type=jnp.float32,
    )
    summed = lax.psum(partial_value, "col")
    weight_parts = []
    for offset in range(ratio):
        weight_parts.append(broadcast(summed, "row", my_col * ratio + offset))
    weight_column = jnp.concatenate(weight_parts, axis=0)
    term = -jnp.dot(
        fitting, weight_column, precision=lax.Precision.HIGHEST, preferred_element_type=jnp.float32
    )
    return lax.psum_scatter(term, "col", scatter_dimension=1, tiled=True)


def solution(mesh):
    in_specs = (P("row", "col"), P(), P("row", "col"), P("row", "col"))
    out_specs = P("row", "col")
    return jax.shard_map(
        per_device, mesh=mesh, in_specs=in_specs, out_specs=out_specs, check_vma=False
    )
```

profile of v0, /device:TPU:0, one launch (start us, length us, event | category | flops | bytes accessed | tf_op | source)
XLA Modules:
  0.0 915.6 jit_solution(14715305341651634228)
XLA Ops:
  6.5 0.0 copy-start
  6.5 0.9 add_select_fusion
  7.5 18.0 %reduce-window.6 = s32[8,8,8,128]{3,2,1,0:T(8,128)S(1)} reduce-window(s32[8,8,8,128]{3,2,1,0:T(8,128)S(1)} %fusion.11, s32[]{:T(128)} %constant.19.clone.1), window={size=1x1x1x128 pad=0_0x0_0x0_0x127_0}, to_apply=%region_0.1 | reduce-window | flops 8323072 | bytes 524292 | tf_op jit(solution)/shard_map/reduce-window
  25.6 1.2 slice_reduce_fusion
  26.8 1.3 reduce-window.9
  28.1 0.1 add_add_fusion
  28.3 0.1 fusion.10
  28.4 2.9 fusion.7
  31.3 4.8 select_reduce_fusion
  36.1 0.0 copy-done
  36.2 8.6 gather_fusion
  44.8 3.2 broadcast_select_fusion.4
  48.0 5.2 all-to-all-start
  53.2 0.0 all-gather.3.cloned.1.call-start
  53.3 26.6 %all-to-all-done = f32[8,256,256]{2,1,0:T(8,128)S(1)} async-done(((f32[8,256,256]{2,1,0:T(8,128)}), f32[8,256,256]{2,1,0:T(8,128)S(1)}, u32[]{:S(2)}, u32[]{:S(2)}) %all-to-all-start) | async-done | bytes 2097184 | tf_op jit(solution)/shard_map/all_to_all | solution.py:35
  79.8 4.7 gather_fusion.1
  84.5 0.0 all-gather.3.cloned.1.call-update
  84.5 0.0 all-reduce.10.cloned.1.call-start
  84.6 80.3 %all-gather.3.cloned.1.call-done = f32[1024,1024]{1,0:T(8,128)} async-done(((f32[1024,256]{1,0:T(8,128)}), f32[1024,1024]{1,0:T(8,128)}) %all-gather.3.cloned.1.call-update) | async-done | bytes 4194320 | tf_op jit(solution)/shard_map/all_gather | solution.py:40
  164.8 6.9 broadcast_select_fusion.2
  171.7 0.0 all-reduce.10.cloned.1.call-update
  171.8 0.2 all-reduce.6.cloned.1.call-start
  172.0 125.3 %all-reduce.10.cloned.1.call-done = (f32[1024,1024]{1,0:T(8,128)}, f32[1024,1024]{1,0:T(8,128)}) async-done(((f32[1024,1024]{1,0:T(8,128)}, f32[1024,1024]{1,0:T(8,128)}), (f32[1024,1024]{1,0:T(8,128)}, f32[1024,1024]{1,0:T(8,128)})) %all-reduce.10.cloned.1.call-update) | async-done | bytes 8388624 | tf_op jit(solution)/shard_map/psum | solution.py:9
  297.3 0.0 copy-start.3
  297.3 2.9 constant_dynamic-update-slice_fusion.1
  300.3 0.5 copy-done.3
  300.8 0.0 copy-start.2
  300.8 0.0 slice-start
  300.8 0.6 constant_dynamic-update-slice_fusion
  301.4 1.6 copy-done.2
  303.0 0.0 slice-start.1
  303.0 27.8 %fusion.17 = f32[1024,2048]{1,0:T(8,128)S(1)} fusion(f32[1024,1024]{1,0:T(8,128)S(1)} %copy-done.2, f32[2048,1024]{1,0:T(8,128)S(1)} %constant_dynamic-update-slice_fusion), kind=kOutput, calls=%fused_computation.44 | convolution fusion | flops 25769803776 | bytes 20971520 | tf_op jit(solution)/shard_map/dot_general | solution.py:45
  330.7 0.0 slice-done
  330.8 0.0 slice-done.1
  330.8 32.1 %fusion.4 = f32[1024,1024]{1,0:T(8,128)} fusion(f32[2048,1024]{1,0:T(8,128)S(1)} %constant_dynamic-update-slice_fusion, f32[1024,2048]{1,0:T(8,128)S(1)} %bitcast.34, f32[1024,2048]{1,0:T(8,128)S(1)} %fusion.17), kind=kOutput, calls=%fused_computation.7 | convolution fusion | flops 25771900928 | bytes 29360128 | tf_op jit(solution)/shard_map/dot_general | solution.py:51
  362.8 0.0 all-reduce.6.cloned.1.call-update
  362.9 0.0 all-reduce.8.cloned.1.call-start
  362.9 155.3 %all-reduce.6.cloned.1.call-done = f32[1024,1024]{1,0:T(8,128)} async-done(((f32[1024,1024]{1,0:T(8,128)}), f32[1024,1024]{1,0:T(8,128)}) %all-reduce.6.cloned.1.call-update) | async-done | bytes 4194320 | tf_op jit(solution)/shard_map/psum | solution.py:57
  518.2 6.9 broadcast_select_fusion.1
  525.1 0.0 all-reduce.8.cloned.1.call-update
  525.1 0.0 reduce-scatter.2.cloned.1.call-start
  525.2 126.0 %all-reduce.8.cloned.1.call-done = (f32[1024,1024]{1,0:T(8,128)}, f32[1024,1024]{1,0:T(8,128)}) async-done(((f32[1024,1024]{1,0:T(8,128)}, f32[1024,1024]{1,0:T(8,128)}), (f32[1024,1024]{1,0:T(8,128)}, f32[1024,1024]{1,0:T(8,128)})) %all-reduce.8.cloned.1.call-update) | async-done | bytes 8388624 | tf_op jit(solution)/shard_map/psum | solution.py:9
  651.2 110.1 %negate_bitcast_fusion = f32[2048,1024]{0,1:T(8,128)} fusion(f32[2048,2048]{1,0:T(8,128)} %param.7, f32[1024,1024]{1,0:T(8,128)} %get-tuple-element.5, f32[1024,1024]{1,0:T(8,128)} %get-tuple-element.6), kind=kOutput, calls=%fused_computation.6 | convolution fusion | flops 51543801856 | bytes 33554432 | tf_op jit(solution)/shard_map/dot_general | solution.py:62
  761.3 0.0 reduce-scatter.2.cloned.1.call-update
  761.3 0.0 copy-start.1
  761.4 144.8 %reduce-scatter.2.cloned.1.call-done = f32[2048,256]{0,1:T(8,128)} async-done(((f32[2048,1024]{0,1:T(8,128)}), f32[2048,256]{0,1:T(8,128)}) %reduce-scatter.2.cloned.1.call-update) | async-done | bytes 2097168 | tf_op jit(solution)/shard_map/reduce_scatter | solution.py:65
  906.2 2.9 copy.7
  909.0 0.0 copy-done.1
  (11 shorter events, 0.1 us)
Async XLA Ops:
  6.5 29.6 %copy-start = (f32[2048,256]{1,0:T(8,128)S(1)}, f32[2048,256]{1,0:T(8,128)}, u32[]{:S(2)}) copy-start(f32[2048,256]{1,0:T(8,128)} %param.4) | copy-start | bytes 6291460
  48.0 31.8 %all-to-all-start = ((f32[8,256,256]{2,1,0:T(8,128)}), f32[8,256,256]{2,1,0:T(8,128)S(1)}, u32[]{:S(2)}, u32[]{:S(2)}) async-start(f32[8,256,256]{2,1,0:T(8,128)} %broadcast_select_fusion.4), calls=%async_computation | async-start | bytes 4194304 | tf_op jit(solution)/shard_map/all_to_all | solution.py:35
  53.2 111.7 %all-gather.3.cloned.1.call-start = ((), (), s32[]{:S(2)}) async-start(), calls=%async_computation.4 | async-start | bytes 5242880 | tf_op jit(solution)/shard_map/all_gather | solution.py:40
  84.5 212.8 %all-reduce.10.cloned.1.call-start = ((), (), s32[]{:S(2)}) async-start(), calls=%async_computation.6 | async-start | bytes 16777216 | tf_op jit(solution)/shard_map/psum | solution.py:9
  171.8 346.4 %all-reduce.6.cloned.1.call-start = ((), (), s32[]{:S(2)}) async-start(), calls=%async_computation.2 | async-start | bytes 8388608 | tf_op jit(solution)/shard_map/psum | solution.py:57
  297.3 3.4 copy-start.3
  300.8 2.2 copy-start.2
  300.8 29.9 %slice-start = ((s8[8388608]{0:T(1024)(128)(4,1)}), s8[4194304]{0:T(1024)(128)(4,1)S(1)}, s32[]{:S(2)}) async-start(s8[8388608]{0:T(1024)(128)(4,1)} %bitcast.33), calls=%async_computation.7 | async-start | bytes 8388608
  303.0 27.8 %slice-start.1 = ((s8[8388608]{0:T(1024)(128)(4,1)}), s8[4194304]{0:T(1024)(128)(4,1)S(1)}, s32[]{:S(2)}) async-start(s8[8388608]{0:T(1024)(128)(4,1)} %bitcast.33), calls=%async_computation.8 | async-start | bytes 8388608
  362.9 288.3 %all-reduce.8.cloned.1.call-start = ((), (), s32[]{:S(2)}) async-start(), calls=%async_computation.5 | async-start | bytes 16777216 | tf_op jit(solution)/shard_map/psum | solution.py:9
  525.1 381.0 %reduce-scatter.2.cloned.1.call-start = ((), (), s32[]{:S(2)}) async-start(), calls=%async_computation.3 | async-start | bytes 10485760 | tf_op jit(solution)/shard_map/reduce_scatter | solution.py:65
  761.3 147.7 %copy-start.1 = (f32[2048,256]{1,0:T(8,128)S(1)}, f32[2048,256]{1,0:T(8,128)}, u32[]{:S(2)}) copy-start(f32[2048,256]{1,0:T(8,128)} %param.4) | copy-start | bytes 6291460
Sparse Core Ops, SparseCore 0:
  84.6 80.1 all-gather.2
  171.9 125.4 all-reduce.9
  363.0 155.1 all-reduce.5
  525.2 125.8 all-reduce.7
  761.5 144.6 reduce-scatter.1
where the time goes:
time: 916 us
  waiting for transfers between devices  658 us (72%)
  matrix products  170 us (19%)
  other arithmetic  45.3 us (5%)
  local copies, waits for them, and re-layouts  23.1 us (3%)
  between operations  13.3 us (1%)
    psum x2, waiting for transfers between devices, broadcast(): return lax.psum(jnp.where(mine, x, jnp.zeros_like(x)), axis)  251 us
    psum x1, waiting for transfers between devices, per_device(): summed = lax.psum(partial_value, 'col')  155 us
    reduce_scatter x1, waiting for transfers between devices, per_device(): return lax.psum_scatter(term, 'col', scatter_dimension=1, tiled=True)  145 us
    dot_general x1, matrix products, per_device(): jnp.dot(fitting, weight_column, precision=lax.Precision.HIGHEST, preferre...  110 us
    all_gather x1, waiting for transfers between devices, per_device(): panel_full = lax.all_gather(panel_strip, 'col', axis=1, tiled=True)  80.3 us
    dot_general x1, matrix products, per_device(): jnp.dot(coulomb * pair, column_full, precision=lax.Precision.HIGHEST, pre...  32.1 us
    dot_general x1, matrix products, per_device(): jnp.dot(panel_full, column_full.T, precision=lax.Precision.HIGHEST, prefe...  27.8 us
    all_to_all x1, waiting for transfers between devices, per_device(): lax.all_to_all(outgoing, 'row', split_axis=0, concat_axis=0, tiled=True)  26.6 us
  transfers between devices with their start and end apart: 6, of which 6 were waited for; matrix products, arithmetic and copies ran while one was open for 0% of the time, Pallas kernels for 0%

commit v1 on v0

v1 whole, which is shorter than its diff:
```python
import jax
import jax.numpy as jnp
from jax import lax
from jax.sharding import PartitionSpec as P


def dot(a, b, contract_b):
    return lax.dot_general(
        a,
        b,
        (((1,), (contract_b,)), ((), ())),
        precision=lax.Precision.HIGH,
        preferred_element_type=jnp.float32,
    )


def split(x):
    high = lax.reduce_precision(x, 8, 7)
    return high.astype(jnp.bfloat16), (x - high).astype(jnp.bfloat16)


def plain(a, b):
    return jnp.dot(a, b, preferred_element_type=jnp.float32)


def per_device(orbitals, point_index, coulomb, fitting):
    rows = lax.axis_size("row")
    cols = lax.axis_size("col")
    ratio = rows // cols
    slab_rows, band_cols = orbitals.shape
    per_panel = point_index.shape[0] // rows
    slots = 2 * per_panel // rows
    my_row = lax.axis_index("row")
    chunks = max(1, band_cols // 128)
    width = band_cols // chunks
    perm = []
    for r in range(rows):
        for c in range(cols):
            perm.append((r * cols + c, ((r % ratio) * cols + c) * cols + r // ratio))

    owner = point_index // slab_rows
    local = (point_index - owner * slab_rows).reshape(rows, per_panel)
    owner = owner.reshape(rows, per_panel)
    mine = owner == my_row
    owner_mine = lax.dynamic_slice_in_dim(owner, my_row, 1, 0)
    held = owner_mine == jnp.arange(rows)[:, None]
    flags = jnp.concatenate([mine, held], axis=0).astype(jnp.bfloat16)
    triangle = (jnp.arange(per_panel)[:, None] <= jnp.arange(per_panel)[None, :]).astype(jnp.bfloat16)
    rank = jnp.dot(flags, triangle, preferred_element_type=jnp.float32).astype(jnp.int32) - 1
    chosen = mine[:, :, None] & (rank[:rows, :, None] == jnp.arange(slots)[None, None, :])
    source = jnp.sum(jnp.where(chosen, local[:, :, None], 0), axis=1)
    slot_mine = jnp.sum(jnp.where(held, rank[rows:], 0), axis=0)

    received = lax.all_to_all(orbitals[source], "row", split_axis=0, concat_axis=0, tiled=True)
    strip = received.reshape(rows * slots, band_cols)[owner_mine[0] * slots + slot_mine]

    def to_column(x):
        held = {0: lax.ppermute(x, ("row", "col"), perm)}
        for d in range(2, rows, 2):
            held[d] = lax.ppermute(held[0], "row", [(r, r ^ d) for r in range(rows)])
        for d in range(0, rows, 2):
            held[d + 1] = lax.ppermute(held[d], "row", [(r, r ^ 1) for r in range(rows)])
        return held

    def lay_out(held):
        w = held[0].shape[1]
        full = jnp.zeros((per_panel, rows * w), jnp.float32)
        for d in range(rows):
            full = lax.dynamic_update_slice(full, held[d], (0, (my_row ^ d) * w))
        return jnp.concatenate([full[:, j * cols * w : (j + 1) * cols * w] for j in range(ratio)], axis=0)

    panel = lax.all_gather(strip, "col", axis=1, tiled=True)
    column = lay_out(to_column(strip))
    pair = dot(panel, column, 1)
    scaled = coulomb * pair
    fitting_high, fitting_low = split(fitting)

    partial = dot(scaled, column, 0)
    outs = []
    for k in range(chunks):
        starts = [c * band_cols + k * width for c in range(cols)]
        part = jnp.concatenate([partial[:, at : at + width] for at in starts], axis=1)
        summed = lax.psum_scatter(part, "col", scatter_dimension=1, tiled=True)
        high, low = split(lay_out(to_column(summed)))
        term = plain(fitting_low, high) + plain(fitting_high, low) + plain(fitting_high, high)
        outs.append(lax.psum_scatter(-term, "col", scatter_dimension=1, tiled=True))
    return jnp.concatenate(outs, axis=1)


def solution(mesh):
    in_specs = (P("row", "col"), P(), P("row", "col"), P("row", "col"))
    return jax.shard_map(
        per_device, mesh=mesh, in_specs=in_specs, out_specs=P("row", "col"), check_vma=False
    )
```

time: 916 us -> 665 us (0.73)
  waiting for transfers between devices: 658 us -> 196 us
  starting transfers between devices: 5.56 us -> 288 us
  matrix products: 170 us -> 101 us
  other arithmetic: 45.3 us -> 21 us
  local copies, waits for them, and re-layouts: 23.1 us -> 36.1 us
    psum x3 -> x0, waiting for transfers between devices: 407 us -> none  [the longest x2 251 us: broadcast(): return lax.psum(jnp.where(mine, x, jnp.zeros_like(x)), axis)]
    ppermute x0 -> x24, starting transfers between devices: none -> 282 us  [the longest x9 170 us: to_column(): held[d] = lax.ppermute(held[0], 'row', [(r, r ^ d) for r in range(rows)])]
    all_gather x1, waiting for transfers between devices: 80.3 us -> 0.01 us  [per_device(): panel = lax.all_gather(strip, 'col', axis=1, tiled=True)]
    dot_general x3 -> x9, matrix products: 170 us -> 101 us  [the longest x2 50.7 us: dot(): lax.dot_general(a, b, (((1,), (contract_b,)), ((), ())), precision=lax.Pr...]
    ppermute x0 -> x24, waiting for transfers between devices: none -> 21.2 us  [the longest x9 19.7 us: to_column(): held[d] = lax.ppermute(held[0], 'row', [(r, r ^ d) for r in range(rows)])]
    another operation x2 -> x0, other arithmetic: 19.3 us -> none
    select_n x4 -> x1, other arithmetic: 17.1 us -> 0.02 us  [per_device(): received.reshape(rows * slots, band_cols)[owner_mine[0] * slots + slot_mine]]
    dynamic_update_slice x0 -> x24, local copies, waits for them, and re-layouts: none -> 12.4 us  [lay_out(): full = lax.dynamic_update_slice(full, held[d], (0, (my_row ^ d) * w))]
  transfers between devices with their start and end apart: 6 -> 30, of which waited for: 6 -> 11; matrix products, arithmetic and copies ran while one was open for 0% -> 12% of each run, Pallas kernels for 0% -> 0%
where the time goes in v1:
time: 665 us; the launch traced here: 656 us
  starting transfers between devices  288 us (43%)
  waiting for transfers between devices  196 us (29%)
  matrix products  101 us (15%)
  local copies, waits for them, and re-layouts  36.1 us (5%)
  other arithmetic  21 us (3%)
  between operations  14.1 us (2%)
    ppermute x9, starting transfers between devices, to_column(): held[d] = lax.ppermute(held[0], 'row', [(r, r ^ d) for r in range(rows)])  170 us
    ppermute x12, starting transfers between devices, to_column(): lax.ppermute(held[d], 'row', [(r, r ^ 1) for r in range(rows)])  96.1 us
    reduce_scatter x2, waiting for transfers between devices, per_device(): outs.append(lax.psum_scatter(-term, 'col', scatter_dimension=1, tiled=True))  85.2 us
    reduce_scatter x2, waiting for transfers between devices, per_device(): summed = lax.psum_scatter(part, 'col', scatter_dimension=1, tiled=True)  62.8 us
    dot_general x2, matrix products, dot(): lax.dot_general(a, b, (((1,), (contract_b,)), ((), ())), precision=lax.Pr...  50.7 us
    dot_general x6, matrix products, plain(): return jnp.dot(a, b, preferred_element_type=jnp.float32)  50 us
    all_to_all x1, waiting for transfers between devices, per_device(): lax.all_to_all(orbitals[source], 'row', split_axis=0, concat_axis=0, tile...  26.6 us
    ppermute x9, waiting for transfers between devices, to_column(): held[d] = lax.ppermute(held[0], 'row', [(r, r ^ d) for r in range(rows)])  19.7 us
  transfers between devices with their start and end apart: 30, of which 11 were waited for; matrix products, arithmetic and copies ran while one was open for 12% of the time, Pallas kernels for 0%

profile of v1, /device:TPU:0, one launch (start us, length us, event | category | flops | bytes accessed | tf_op | source)
XLA Modules:
  0.0 655.6 jit_solution(2838118695921094714)
XLA Ops:
  7.9 4.8 select_reduce_fusion
  12.8 8.6 %gather_fusion = f32[2048,256]{1,0:T(8,128)} fusion(f32[2048,256]{1,0:T(8,128)S(1)} %copy-done, s32[2048]{0:T(1024)S(1)} %broadcast_clamp_fusion), kind=kCustom, calls=%fused_computation | custom fusion | bytes 4202496 | tf_op jit(solution)/shard_map/gather | solution.py:54
  21.4 5.2 all-to-all-start
  26.6 26.6 %all-to-all-done = f32[8,256,256]{2,1,0:T(8,128)S(1)} async-done(((f32[8,256,256]{2,1,0:T(8,128)}), f32[8,256,256]{2,1,0:T(8,128)S(1)}, u32[]{:S(2)}, u32[]{:S(2)}) %all-to-all-start) | async-done | bytes 2097184 | tf_op jit(solution)/shard_map/all_to_all | solution.py:54
  53.2 4.7 gather_fusion.1
  58.0 9.5 %collective-permute-start = (f32[1024,256]{1,0:T(8,128)}, f32[1024,256]{1,0:T(8,128)}, u32[]{:S(2)}, u32[]{:S(2)}) collective-permute-start(f32[1024,256]{1,0:T(8,128)} %gather_fusion.1), channel_id=1, source_target_pairs={{0,0},{1,4},{2,8},{3,12},{4,16},{5,20},{6,24},{7,28},{8,1},{9,5},{... | collective-permute-start | bytes 3145736 | tf_op jit(solution)/shard_map/ppermute | solution.py:58
  67.5 99.7 %collective-permute-start.2 = (f32[1024,256]{1,0:T(8,128)}, f32[1024,256]{1,0:T(8,128)S(1)}, u32[]{:S(2)}, u32[]{:S(2)}) collective-permute-start(f32[1024,256]{1,0:T(8,128)} %collective-permute-done), channel_id=1, source_target_pairs={{0,8},{4,12},{8,0},{12,4},{16,24},{20,28},{24,16},{28,20},{1,9},{5... | collective-permute-start | bytes 3145736 | tf_op jit(solution)/shard_map/ppermute | solution.py:60
  168.6 17.4 %collective-permute-start.1 = (f32[1024,256]{1,0:T(8,128)}, f32[1024,256]{1,0:T(8,128)}, u32[]{:S(2)}, u32[]{:S(2)}) collective-permute-start(f32[1024,256]{1,0:T(8,128)} %collective-permute-done), channel_id=1, source_target_pairs={{0,4},{4,0},{8,12},{12,8},{16,20},{20,16},{24,28},{28,24},{1,5},{5... | collective-permute-start | bytes 3145736 | tf_op jit(solution)/shard_map/ppermute | solution.py:62
  186.0 16.8 %collective-permute-start.3 = (f32[1024,256]{1,0:T(8,128)S(1)}, f32[1024,256]{1,0:T(8,128)}, u32[]{:S(2)}, u32[]{:S(2)}) collective-permute-start(f32[1024,256]{1,0:T(8,128)S(1)} %collective-permute-done.2), channel_id=1, source_target_pairs={{0,4},{4,0},{8,12},{12,8},{16,20},{20,16},{24,28},{28,24},{1,5},{5... | collective-permute-start | bytes 3145736 | tf_op jit(solution)/shard_map/ppermute | solution.py:62
  202.8 3.7 collective-permute-done.4
  206.5 9.2 %collective-permute-start.5 = (f32[1024,256]{1,0:T(8,128)S(1)}, f32[1024,256]{1,0:T(8,128)}, u32[]{:S(2)}, u32[]{:S(2)}) collective-permute-start(f32[1024,256]{1,0:T(8,128)S(1)} %collective-permute-done.4), channel_id=1, source_target_pairs={{0,4},{4,0},{8,12},{12,8},{16,20},{20,16},{24,28},{28,24},{1,5},{5... | collective-permute-start | bytes 3145736 | tf_op jit(solution)/shard_map/ppermute | solution.py:62
  216.7 1.4 constant_dynamic-update-slice_fusion.21
  218.1 1.4 constant_dynamic-update-slice_fusion.20
  219.6 1.4 constant_dynamic-update-slice_fusion.18
  221.1 1.4 constant_dynamic-update-slice_fusion.16
  222.6 1.4 constant_dynamic-update-slice_fusion.14
  224.0 4.1 fusion.36
  228.1 19.4 %fusion.4 = f32[1024,2048]{1,0:T(8,128)} fusion(f32[1024,1024]{1,0:T(8,128)} %all-gather.3.cloned.1.call-done, f32[1024,1024]{1,0:T(8,128)} %get-tuple-element.6, f32[1024,1024]{1,0:T(8,128)} %get-tuple-element.5), kind=kOutput, calls=%fused_computation.11 | convolution fusion | flops 12886999040 | bytes 20971520 | tf_op jit(solution)/shard_map/dot_general | solution.py:8
  247.5 31.3 %fusion.1 = f32[1024,1024]{0,1:T(8,128)S(1)} fusion(f32[1024,2048]{1,0:T(8,128)} %param.6, f32[1024,2048]{1,0:T(8,128)} %fusion.4, f32[1024,1024]{1,0:T(8,128)S(1)} %copy-done.3, f32[1024,1024]{1,0:T(8,128)S(1)} %copy-done.2), kind=kOutput, calls=%fused_computation.6 | convolution fusion | flops 12889096192 | bytes 29360128 | tf_op jit(solution)/shard_map/dot_general | solution.py:8
  279.2 1.5 pad_maximum_fusion.5
  280.8 60.1 %reduce-scatter.5.cloned.1.call-done = f32[1024,128]{0,1:T(8,128)} async-done(((f32[1024,512]{0,1:T(8,128)}), f32[1024,128]{0,1:T(8,128)}) %reduce-scatter.5.cloned.1.call-update) | async-done | bytes 524304 | tf_op jit(solution)/shard_map/reduce_scatter | solution.py:83
  340.8 5.4 collective-permute-start.8
  346.2 32.9 %collective-permute-start.9 = (f32[1024,128]{0,1:T(8,128)}, f32[1024,128]{0,1:T(8,128)}, u32[]{:S(2)}, u32[]{:S(2)}) collective-permute-start(f32[1024,128]{0,1:T(8,128)} %collective-permute-done.8), channel_id=1, source_target_pairs={{0,4},{4,0},{8,12},{12,8},{16,20},{20,16},{24,28},{28,24},{1,5},{5... | collective-permute-start | bytes 1572872 | tf_op jit(solution)/shard_map/ppermute | solution.py:62
  379.1 1.8 collective-permute-start.12
  380.9 1.7 collective-permute-start.14
  382.6 9.1 %reduce-precision_convert_fusion = bf16[2048,2048]{1,0:T(8,128)(2,1)} fusion(f32[2048,2048]{1,0:T(8,128)} %param.7), kind=kLoop, calls=%fused_computation.2 | loop fusion | flops 8388608 | bytes 25165824 | tf_op jit(solution)/shard_map/convert_element_type | solution.py:19
  391.7 2.5 collective-permute-done.10
  394.2 1.6 pad_maximum_fusion.6
  395.8 8.0 %collective-permute-done.12 = f32[1024,128]{0,1:T(8,128)S(1)} collective-permute-done((f32[1024,128]{0,1:T(8,128)}, f32[1024,128]{0,1:T(8,128)S(1)}, u32[]{:S(2)}, u32[]{:S(2)}) %collective-permute-start.12) | collective-permute-done | bytes 524320 | tf_op jit(solution)/shard_map/ppermute | solution.py:60
  407.2 1.3 constant_dynamic-update-slice_fusion.11
  410.2 1.9 slice-done.1
  412.1 6.3 fusion.16
  418.4 10.2 %fusion.12 = f32[2048,512]{1,0:T(8,128)} fusion(f32[2048,2048]{1,0:T(8,128)} %param.7, f32[1024,512]{0,1:T(8,128)S(1)} %get-tuple-element.8, f32[1024,512]{0,1:T(8,128)S(1)} %get-tuple-element.7), kind=kOutput, calls=%fused_computation.29 | convolution fusion | flops 4310695936 | bytes 25165824 | tf_op jit(solution)/shard_map/dot_general | solution.py:23
  428.7 8.3 %fusion.8 = f32[2048,512]{1,0:T(8,128)} fusion(f32[2048,512]{1,0:T(8,128)} %fusion.12, f32[512,2048]{0,1:T(8,128)} %fusion.16, bf16[2048,2048]{1,0:T(8,128)(2,1)S(1)} %bitcast.38, f32[1024,512]{0,1:T(8,128)S(1)} %get-tuple-element.8, f32[1024,512]{0,1:T(8,128)S(1)} %get-tuple-element.7), kind=kOutput, calls=%fused_computation.24 | convolution fusion | flops 4301258752 | bytes 25165824 | tf_op jit(solution)/shard_map/dot_general | solution.py:23
  437.1 2.7 reduce-scatter.9.cloned.1.call-done
  439.8 1.7 collective-permute-start.16
  441.5 62.7 %collective-permute-start.18 = (f32[1024,128]{0,1:T(8,128)S(1)}, f32[1024,128]{0,1:T(8,128)S(1)}, u32[]{:S(2)}, u32[]{:S(2)}) collective-permute-start(f32[1024,128]{0,1:T(8,128)S(1)} %collective-permute-done.16), channel_id=1, source_target_pairs={{0,8},{4,12},{8,0},{12,4},{16,24},{20,28},{24,16},{28,20},{1,9},{5... | collective-permute-start | bytes 1572872 | tf_op jit(solution)/shard_map/ppermute | solution.py:60
  504.2 2.3 collective-permute-start.20
  506.4 8.6 %collective-permute-start.17 = (f32[1024,128]{0,1:T(8,128)S(1)}, f32[1024,128]{0,1:T(8,128)S(1)}, u32[]{:S(2)}, u32[]{:S(2)}) collective-permute-start(f32[1024,128]{0,1:T(8,128)S(1)} %collective-permute-done.16), channel_id=1, source_target_pairs={{0,4},{4,0},{8,12},{12,8},{16,20},{20,16},{24,28},{28,24},{1,5},{5... | collective-permute-start | bytes 1572872 | tf_op jit(solution)/shard_map/ppermute | solution.py:62
  515.0 8.2 %collective-permute-start.19 = (f32[1024,128]{0,1:T(8,128)S(1)}, f32[1024,128]{0,1:T(8,128)S(1)}, u32[]{:S(2)}, u32[]{:S(2)}) collective-permute-start(f32[1024,128]{0,1:T(8,128)S(1)} %collective-permute-done.18), channel_id=1, source_target_pairs={{0,4},{4,0},{8,12},{12,8},{16,20},{20,16},{24,28},{28,24},{1,5},{5... | collective-permute-start | bytes 1572872 | tf_op jit(solution)/shard_map/ppermute | solution.py:62
  523.2 5.3 collective-permute-done.20
  528.5 2.7 collective-permute-start.21
  534.1 1.3 slice-done.3
  535.4 6.3 fusion.14
  541.7 10.3 %fusion.10 = f32[2048,512]{1,0:T(8,128)} fusion(f32[2048,2048]{1,0:T(8,128)} %param.7, f32[1024,512]{0,1:T(8,128)S(1)} %get-tuple-element.18, f32[1024,512]{0,1:T(8,128)S(1)} %get-tuple-element.17), kind=kOutput, calls=%fused_computation.28 | convolution fusion | flops 4310695936 | bytes 25165824 | tf_op jit(solution)/shard_map/dot_general | solution.py:23
  552.0 8.4 %fusion.7 = f32[2048,512]{1,0:T(8,128)} fusion(f32[2048,512]{1,0:T(8,128)} %fusion.10, f32[512,2048]{0,1:T(8,128)} %fusion.14, bf16[2048,2048]{1,0:T(8,128)(2,1)S(1)} %bitcast.40, f32[1024,512]{0,1:T(8,128)S(1)} %get-tuple-element.18, f32[1024,512]{0,1:T(8,128)S(1)} %get-tuple-element.17), kind=kOutput, calls=%fused_computation.21 | convolution fusion | flops 4301258752 | bytes 25165824 | tf_op jit(solution)/shard_map/dot_general | solution.py:23
  560.5 85.2 %reduce-scatter.11.cloned.1.call-done = f32[2048,128]{1,0:T(8,128)} async-done(((f32[2048,512]{1,0:T(8,128)}), f32[2048,128]{1,0:T(8,128)}) %reduce-scatter.11.cloned.1.call-update) | async-done | bytes 1048592 | tf_op jit(solution)/shard_map/reduce_scatter | solution.py:86
  645.7 3.0 pad_maximum_fusion.7
  (93 shorter events, 12.9 us)
Async XLA Ops:
  6.5 6.2 copy-start
  21.4 31.8 %all-to-all-start = ((f32[8,256,256]{2,1,0:T(8,128)}), f32[8,256,256]{2,1,0:T(8,128)S(1)}, u32[]{:S(2)}, u32[]{:S(2)}) async-start(f32[8,256,256]{2,1,0:T(8,128)} %bitcast.41), calls=%async_computation | async-start | bytes 4194304 | tf_op jit(solution)/shard_map/all_to_all | solution.py:54
  26.6 201.5 %all-gather.3.cloned.1.call-start = ((), (), s32[]{:S(2)}) async-start(), calls=%async_computation.9 | async-start | bytes 5242880 | tf_op jit(solution)/shard_map/all_gather | solution.py:72
  57.9 282.9 %reduce-scatter.5.cloned.1.call-start = ((), (), s32[]{:S(2)}) async-start(), calls=%async_computation.5 | async-start | bytes 2621440 | tf_op jit(solution)/shard_map/reduce_scatter | solution.py:83
  58.0 9.5 %collective-permute-start = (f32[1024,256]{1,0:T(8,128)}, f32[1024,256]{1,0:T(8,128)}, u32[]{:S(2)}, u32[]{:S(2)}) collective-permute-start(f32[1024,256]{1,0:T(8,128)} %gather_fusion.1), channel_id=1, source_target_pairs={{0,0},{1,4},{2,8},{3,12},{4,16},{5,20},{6,24},{7,28},{8,1},{9,5},{... | collective-permute-start | bytes 3145736 | tf_op jit(solution)/shard_map/ppermute | solution.py:58
  67.5 118.6 %collective-permute-start.2 = (f32[1024,256]{1,0:T(8,128)}, f32[1024,256]{1,0:T(8,128)S(1)}, u32[]{:S(2)}, u32[]{:S(2)}) collective-permute-start(f32[1024,256]{1,0:T(8,128)} %collective-permute-done), channel_id=1, source_target_pairs={{0,8},{4,12},{8,0},{12,4},{16,24},{20,28},{24,16},{28,20},{1,9},{5... | collective-permute-start | bytes 3145736 | tf_op jit(solution)/shard_map/ppermute | solution.py:60
  167.2 39.3 %collective-permute-start.4 = (f32[1024,256]{1,0:T(8,128)}, f32[1024,256]{1,0:T(8,128)S(1)}, u32[]{:S(2)}, u32[]{:S(2)}) collective-permute-start(f32[1024,256]{1,0:T(8,128)} %collective-permute-done), channel_id=1, source_target_pairs={{0,16},{4,20},{8,24},{12,28},{16,0},{20,4},{24,8},{28,12},{1,17},{... | collective-permute-start | bytes 3145736 | tf_op jit(solution)/shard_map/ppermute | solution.py:60
  167.7 48.0 %collective-permute-start.6 = (f32[1024,256]{1,0:T(8,128)}, f32[1024,256]{1,0:T(8,128)S(1)}, u32[]{:S(2)}, u32[]{:S(2)}) collective-permute-start(f32[1024,256]{1,0:T(8,128)} %collective-permute-done), channel_id=1, source_target_pairs={{0,24},{4,28},{8,16},{12,20},{16,8},{20,12},{24,0},{28,4},{1,25},{... | collective-permute-start | bytes 3145736 | tf_op jit(solution)/shard_map/ppermute | solution.py:60
  168.6 49.5 %collective-permute-start.1 = (f32[1024,256]{1,0:T(8,128)}, f32[1024,256]{1,0:T(8,128)}, u32[]{:S(2)}, u32[]{:S(2)}) collective-permute-start(f32[1024,256]{1,0:T(8,128)} %collective-permute-done), channel_id=1, source_target_pairs={{0,4},{4,0},{8,12},{12,8},{16,20},{20,16},{24,28},{28,24},{1,5},{5... | collective-permute-start | bytes 3145736 | tf_op jit(solution)/shard_map/ppermute | solution.py:62
  186.0 33.6 %collective-permute-start.3 = (f32[1024,256]{1,0:T(8,128)S(1)}, f32[1024,256]{1,0:T(8,128)}, u32[]{:S(2)}, u32[]{:S(2)}) collective-permute-start(f32[1024,256]{1,0:T(8,128)S(1)} %collective-permute-done.2), channel_id=1, source_target_pairs={{0,4},{4,0},{8,12},{12,8},{16,20},{20,16},{24,28},{28,24},{1,5},{5... | collective-permute-start | bytes 3145736 | tf_op jit(solution)/shard_map/ppermute | solution.py:62
  206.5 14.6 %collective-permute-start.5 = (f32[1024,256]{1,0:T(8,128)S(1)}, f32[1024,256]{1,0:T(8,128)}, u32[]{:S(2)}, u32[]{:S(2)}) collective-permute-start(f32[1024,256]{1,0:T(8,128)S(1)} %collective-permute-done.4), channel_id=1, source_target_pairs={{0,4},{4,0},{8,12},{12,8},{16,20},{20,16},{24,28},{28,24},{1,5},{5... | collective-permute-start | bytes 3145736 | tf_op jit(solution)/shard_map/ppermute | solution.py:62
  215.7 6.9 %collective-permute-start.7 = (f32[1024,256]{1,0:T(8,128)S(1)}, f32[1024,256]{1,0:T(8,128)}, u32[]{:S(2)}, u32[]{:S(2)}) collective-permute-start(f32[1024,256]{1,0:T(8,128)S(1)} %collective-permute-done.6), channel_id=1, source_target_pairs={{0,4},{4,0},{8,12},{12,8},{16,20},{20,16},{24,28},{28,24},{1,5},{5... | collective-permute-start | bytes 3145736 | tf_op jit(solution)/shard_map/ppermute | solution.py:62
  228.1 19.4 %copy-start.2 = (f32[1024,1024]{1,0:T(8,128)S(1)}, f32[1024,1024]{1,0:T(8,128)}, u32[]{:S(2)}) copy-start(f32[1024,1024]{1,0:T(8,128)} %get-tuple-element.5) | copy-start | bytes 12582916
  228.1 19.4 %copy-start.3 = (f32[1024,1024]{1,0:T(8,128)S(1)}, f32[1024,1024]{1,0:T(8,128)}, u32[]{:S(2)}) copy-start(f32[1024,1024]{1,0:T(8,128)} %get-tuple-element.6) | copy-start | bytes 12582916
  280.7 159.1 %reduce-scatter.9.cloned.1.call-start = ((), (), s32[]{:S(2)}) async-start(), calls=%async_computation.7 | async-start | bytes 2621440 | tf_op jit(solution)/shard_map/reduce_scatter | solution.py:83
  340.8 5.4 collective-permute-start.8
  346.2 59.8 %collective-permute-start.9 = (f32[1024,128]{0,1:T(8,128)}, f32[1024,128]{0,1:T(8,128)}, u32[]{:S(2)}, u32[]{:S(2)}) collective-permute-start(f32[1024,128]{0,1:T(8,128)} %collective-permute-done.8), channel_id=1, source_target_pairs={{0,4},{4,0},{8,12},{12,8},{16,20},{20,16},{24,28},{28,24},{1,5},{5... | collective-permute-start | bytes 1572872 | tf_op jit(solution)/shard_map/ppermute | solution.py:62
  379.1 15.1 %collective-permute-start.10 = (f32[1024,128]{0,1:T(8,128)}, f32[1024,128]{0,1:T(8,128)}, u32[]{:S(2)}, u32[]{:S(2)}) collective-permute-start(f32[1024,128]{0,1:T(8,128)} %collective-permute-done.8), channel_id=1, source_target_pairs={{0,8},{4,12},{8,0},{12,4},{16,24},{20,28},{24,16},{28,20},{1,9},{5... | collective-permute-start | bytes 1572872 | tf_op jit(solution)/shard_map/ppermute | solution.py:60
  379.1 24.7 %collective-permute-start.12 = (f32[1024,128]{0,1:T(8,128)}, f32[1024,128]{0,1:T(8,128)S(1)}, u32[]{:S(2)}, u32[]{:S(2)}) collective-permute-start(f32[1024,128]{0,1:T(8,128)} %collective-permute-done.8), channel_id=1, source_target_pairs={{0,16},{4,20},{8,24},{12,28},{16,0},{20,4},{24,8},{28,12},{1,17},{... | collective-permute-start | bytes 1572872 | tf_op jit(solution)/shard_map/ppermute | solution.py:60
  380.9 24.7 %collective-permute-start.14 = (f32[1024,128]{0,1:T(8,128)}, f32[1024,128]{0,1:T(8,128)S(1)}, u32[]{:S(2)}, u32[]{:S(2)}) collective-permute-start(f32[1024,128]{0,1:T(8,128)} %collective-permute-done.8), channel_id=1, source_target_pairs={{0,24},{4,28},{8,16},{12,20},{16,8},{20,12},{24,0},{28,4},{1,25},{... | collective-permute-start | bytes 1572872 | tf_op jit(solution)/shard_map/ppermute | solution.py:60
  394.2 14.3 %collective-permute-start.11 = (f32[1024,128]{0,1:T(8,128)}, f32[1024,128]{0,1:T(8,128)}, u32[]{:S(2)}, u32[]{:S(2)}) collective-permute-start(f32[1024,128]{0,1:T(8,128)} %collective-permute-done.10), channel_id=1, source_target_pairs={{0,4},{4,0},{8,12},{12,8},{16,20},{20,16},{24,28},{28,24},{1,5},{5... | collective-permute-start | bytes 1572872 | tf_op jit(solution)/shard_map/ppermute | solution.py:62
  395.8 164.7 %reduce-scatter.7.cloned.1.call-start = ((), (), s32[]{:S(2)}) async-start(), calls=%async_computation.6 | async-start | bytes 5242880 | tf_op jit(solution)/shard_map/reduce_scatter | solution.py:86
  403.8 5.9 collective-permute-start.13
  405.6 4.2 collective-permute-start.15
  406.0 4.2 slice-start
  409.9 2.2 slice-start.1
  437.0 208.7 %reduce-scatter.11.cloned.1.call-start = ((), (), s32[]{:S(2)}) async-start(), calls=%async_computation.8 | async-start | bytes 5242880 | tf_op jit(solution)/shard_map/reduce_scatter | solution.py:86
  439.8 1.7 collective-permute-start.16
  441.5 73.5 %collective-permute-start.18 = (f32[1024,128]{0,1:T(8,128)S(1)}, f32[1024,128]{0,1:T(8,128)S(1)}, u32[]{:S(2)}, u32[]{:S(2)}) collective-permute-start(f32[1024,128]{0,1:T(8,128)S(1)} %collective-permute-done.16), channel_id=1, source_target_pairs={{0,8},{4,12},{8,0},{12,4},{16,24},{20,28},{24,16},{28,20},{1,9},{5... | collective-permute-start | bytes 1572872 | tf_op jit(solution)/shard_map/ppermute | solution.py:60
  504.2 24.3 %collective-permute-start.20 = (f32[1024,128]{0,1:T(8,128)S(1)}, f32[1024,128]{0,1:T(8,128)S(1)}, u32[]{:S(2)}, u32[]{:S(2)}) collective-permute-start(f32[1024,128]{0,1:T(8,128)S(1)} %collective-permute-done.16), channel_id=1, source_target_pairs={{0,16},{4,20},{8,24},{12,28},{16,0},{20,4},{24,8},{28,12},{1,17},{... | collective-permute-start | bytes 1572872 | tf_op jit(solution)/shard_map/ppermute | solution.py:60
  506.4 25.3 %collective-permute-start.22 = (f32[1024,128]{0,1:T(8,128)S(1)}, f32[1024,128]{0,1:T(8,128)S(1)}, u32[]{:S(2)}, u32[]{:S(2)}) collective-permute-start(f32[1024,128]{0,1:T(8,128)S(1)} %collective-permute-done.16), channel_id=1, source_target_pairs={{0,24},{4,28},{8,16},{12,20},{16,8},{20,12},{24,0},{28,4},{1,25},{... | collective-permute-start | bytes 1572872 | tf_op jit(solution)/shard_map/ppermute | solution.py:60
  506.4 25.4 %collective-permute-start.17 = (f32[1024,128]{0,1:T(8,128)S(1)}, f32[1024,128]{0,1:T(8,128)S(1)}, u32[]{:S(2)}, u32[]{:S(2)}) collective-permute-start(f32[1024,128]{0,1:T(8,128)S(1)} %collective-permute-done.16), channel_id=1, source_target_pairs={{0,4},{4,0},{8,12},{12,8},{16,20},{20,16},{24,28},{28,24},{1,5},{5... | collective-permute-start | bytes 1572872 | tf_op jit(solution)/shard_map/ppermute | solution.py:62
  515.0 16.9 %collective-permute-start.19 = (f32[1024,128]{0,1:T(8,128)S(1)}, f32[1024,128]{0,1:T(8,128)S(1)}, u32[]{:S(2)}, u32[]{:S(2)}) collective-permute-start(f32[1024,128]{0,1:T(8,128)S(1)} %collective-permute-done.18), channel_id=1, source_target_pairs={{0,4},{4,0},{8,12},{12,8},{16,20},{20,16},{24,28},{28,24},{1,5},{5... | collective-permute-start | bytes 1572872 | tf_op jit(solution)/shard_map/ppermute | solution.py:62
  528.5 4.2 collective-permute-start.21
  531.7 2.4 slice-start.2
  531.7 2.0 collective-permute-start.23
  532.8 2.6 slice-start.3
  560.5 88.2 %copy-start.1 = (f32[2048,256]{1,0:T(8,128)S(1)}, f32[2048,256]{1,0:T(8,128)}, u32[]{:S(2)}) copy-start(f32[2048,256]{1,0:T(8,128)} %param.4) | copy-start | bytes 6291460
Sparse Core Ops, SparseCore 0:
  58.0 137.6 all-gather.2
  280.8 59.9 reduce-scatter.4
  395.9 43.8 reduce-scatter.8
  442.0 106.2 reduce-scatter.6
  560.6 85.0 reduce-scatter.10

commit v2 on v1

--- a/solution.py
+++ b/solution.py
@@ -33,6 +33,7 @@
     my_row = lax.axis_index("row")
     chunks = max(1, band_cols // 128)
     width = band_cols // chunks
+    wide = width * cols
     perm = []
     for r in range(rows):
         for c in range(cols):
@@ -62,26 +63,28 @@
             held[d + 1] = lax.ppermute(held[d], "row", [(r, r ^ 1) for r in range(rows)])
         return held
 
-    def lay_out(held):
-        w = held[0].shape[1]
-        full = jnp.zeros((per_panel, rows * w), jnp.float32)
+    def lay_out(held, start):
+        full = jnp.zeros((per_panel, rows * width), jnp.float32)
         for d in range(rows):
-            full = lax.dynamic_update_slice(full, held[d], (0, (my_row ^ d) * w))
-        return jnp.concatenate([full[:, j * cols * w : (j + 1) * cols * w] for j in range(ratio)], axis=0)
+            part = held[d][:, start : start + width]
+            full = lax.dynamic_update_slice(full, part, (0, (my_row ^ d) * width))
+        return jnp.concatenate([full[:, j * wide : (j + 1) * wide] for j in range(ratio)], axis=0)
 
+    arrived = to_column(strip)
+    column = [lay_out(arrived, k * width) for k in range(chunks)]
     panel = lax.all_gather(strip, "col", axis=1, tiled=True)
-    column = lay_out(to_column(strip))
-    pair = dot(panel, column, 1)
+    panel = panel.reshape(per_panel, cols, chunks, width)
+    pair = 0
+    for k in range(chunks):
+        pair = pair + dot(panel[:, :, k].reshape(per_panel, wide), column[k], 1)
     scaled = coulomb * pair
     fitting_high, fitting_low = split(fitting)
 
-    partial = dot(scaled, column, 0)
     outs = []
     for k in range(chunks):
-        starts = [c * band_cols + k * width for c in range(cols)]
-        part = jnp.concatenate([partial[:, at : at + width] for at in starts], axis=1)
-        summed = lax.psum_scatter(part, "col", scatter_dimension=1, tiled=True)
-        high, low = split(lay_out(to_column(summed)))
+        partial = dot(scaled, column[k], 0)
+        summed = lax.psum_scatter(partial, "col", scatter_dimension=1, tiled=True)
+        high, low = split(lay_out(to_column(summed), 0))
         term = plain(fitting_low, high) + plain(fitting_high, low) + plain(fitting_high, high)
         outs.append(lax.psum_scatter(-term, "col", scatter_dimension=1, tiled=True))
     return jnp.concatenate(outs, axis=1)

time: 665 us -> 632 us (0.950)
  starting transfers between devices: 288 us -> 264 us
  local copies, waits for them, and re-layouts: 36.1 us -> 51.6 us
  matrix products: 101 us -> 89.2 us
  waiting for transfers between devices: 196 us -> 187 us
    reduce_scatter x2, waiting for transfers between devices: 85.2 us -> 102 us  [per_device(): outs.append(lax.psum_scatter(-term, 'col', scatter_dimension=1, tiled=True))]
    ppermute x12, starting transfers between devices: 96.1 us -> 80.5 us  [to_column(): lax.ppermute(held[d], 'row', [(r, r ^ 1) for r in range(rows)])]
    slice x4 -> x5, local copies, waits for them, and re-layouts: 5.14 us -> 20.5 us  [the longest x1 15.1 us: per_device(): pair = pair + dot(panel[:, :, k].reshape(per_panel, wide), column[k], 1)]
    ppermute x9, waiting for transfers between devices: 19.7 us -> 6.73 us  [to_column(): held[d] = lax.ppermute(held[0], 'row', [(r, r ^ d) for r in range(rows)])]
    reduce_scatter x2, waiting for transfers between devices: 62.8 us -> 49.9 us  [per_device(): summed = lax.psum_scatter(partial, 'col', scatter_dimension=1, tiled=True)]
    dot_general x2 -> x4, matrix products: 50.7 us -> 41 us  [dot(): lax.dot_general(a, b, (((1,), (contract_b,)), ((), ())), precision=lax.Pr...]
  transfers between devices with their start and end apart: 30 -> 30, of which waited for: 11 -> 8; matrix products, arithmetic and copies ran while one was open for 12% -> 13% of each run, Pallas kernels for 0% -> 0%
where the time goes in v2:
time: 632 us; the launch traced here: 624 us
  starting transfers between devices  264 us (42%)
  waiting for transfers between devices  187 us (30%)
  matrix products  89.2 us (14%)
  local copies, waits for them, and re-layouts  51.6 us (8%)
  other arithmetic  17.9 us (3%)
  between operations  14.2 us (2%)
    ppermute x9, starting transfers between devices, to_column(): held[d] = lax.ppermute(held[0], 'row', [(r, r ^ d) for r in range(rows)])  165 us
    reduce_scatter x2, waiting for transfers between devices, per_device(): outs.append(lax.psum_scatter(-term, 'col', scatter_dimension=1, tiled=True))  102 us
    ppermute x12, starting transfers between devices, to_column(): lax.ppermute(held[d], 'row', [(r, r ^ 1) for r in range(rows)])  80.5 us
    reduce_scatter x2, waiting for transfers between devices, per_device(): summed = lax.psum_scatter(partial, 'col', scatter_dimension=1, tiled=True)  49.9 us
    dot_general x6, matrix products, plain(): return jnp.dot(a, b, preferred_element_type=jnp.float32)  47.8 us
    dot_general x4, matrix products, dot(): lax.dot_general(a, b, (((1,), (contract_b,)), ((), ())), precision=lax.Pr...  41 us
    all_to_all x1, waiting for transfers between devices, per_device(): lax.all_to_all(orbitals[source], 'row', split_axis=0, concat_axis=0, tile...  26.6 us
    slice x1, local copies, waits for them, and re-layouts, per_device(): pair = pair + dot(panel[:, :, k].reshape(per_panel, wide), column[k], 1)  15.1 us
  transfers between devices with their start and end apart: 30, of which 8 were waited for; matrix products, arithmetic and copies ran while one was open for 13% of the time, Pallas kernels for 0%

profile of v2, /device:TPU:0, one launch (start us, length us, event | category | flops | bytes accessed | tf_op | source)
XLA Modules:
  0.0 623.9 jit_solution(18173620713505954981)
XLA Ops:
  7.9 4.8 select_reduce_fusion
  12.8 8.6 %gather_fusion = f32[2048,256]{1,0:T(8,128)} fusion(f32[2048,256]{1,0:T(8,128)S(1)} %copy-done, s32[2048]{0:T(1024)S(1)} %broadcast_clamp_fusion), kind=kCustom, calls=%fused_computation | custom fusion | bytes 4202496 | tf_op jit(solution)/shard_map/gather | solution.py:55
  21.4 5.2 all-to-all-start
  26.6 26.6 %all-to-all-done = f32[8,256,256]{2,1,0:T(8,128)S(1)} async-done(((f32[8,256,256]{2,1,0:T(8,128)}), f32[8,256,256]{2,1,0:T(8,128)S(1)}, u32[]{:S(2)}, u32[]{:S(2)}) %all-to-all-start) | async-done | bytes 2097184 | tf_op jit(solution)/shard_map/all_to_all | solution.py:55
  53.2 4.7 gather_fusion.1
  58.0 9.5 %collective-permute-start = (f32[1024,256]{1,0:T(8,128)}, f32[1024,256]{1,0:T(8,128)}, u32[]{:S(2)}, u32[]{:S(2)}) collective-permute-start(f32[1024,256]{1,0:T(8,128)} %gather_fusion.1), channel_id=1, source_target_pairs={{0,0},{1,4},{2,8},{3,12},{4,16},{5,20},{6,24},{7,28},{8,1},{9,5},{... | collective-permute-start | bytes 3145736 | tf_op jit(solution)/shard_map/ppermute | solution.py:59
  67.5 99.7 %collective-permute-start.2 = (f32[1024,256]{1,0:T(8,128)}, f32[1024,256]{1,0:T(8,128)S(1)}, u32[]{:S(2)}, u32[]{:S(2)}) collective-permute-start(f32[1024,256]{1,0:T(8,128)} %collective-permute-done), channel_id=1, source_target_pairs={{0,8},{4,12},{8,0},{12,4},{16,24},{20,28},{24,16},{28,20},{1,9},{5... | collective-permute-start | bytes 3145736 | tf_op jit(solution)/shard_map/ppermute | solution.py:61
  167.2 1.5 collective-permute-start.4
  168.7 17.4 %collective-permute-start.1 = (f32[1024,256]{1,0:T(8,128)}, f32[1024,256]{1,0:T(8,128)}, u32[]{:S(2)}, u32[]{:S(2)}) collective-permute-start(f32[1024,256]{1,0:T(8,128)} %collective-permute-done), channel_id=1, source_target_pairs={{0,4},{4,0},{8,12},{12,8},{16,20},{20,16},{24,28},{28,24},{1,5},{5... | collective-permute-start | bytes 3145736 | tf_op jit(solution)/shard_map/ppermute | solution.py:63
  186.0 16.8 %collective-permute-start.3 = (f32[1024,256]{1,0:T(8,128)S(1)}, f32[1024,256]{1,0:T(8,128)}, u32[]{:S(2)}, u32[]{:S(2)}) collective-permute-start(f32[1024,256]{1,0:T(8,128)S(1)} %collective-permute-done.2), channel_id=1, source_target_pairs={{0,4},{4,0},{8,12},{12,8},{16,20},{20,16},{24,28},{28,24},{1,5},{5... | collective-permute-start | bytes 3145736 | tf_op jit(solution)/shard_map/ppermute | solution.py:63
  206.1 7.6 %collective-permute-start.7 = (f32[1024,256]{1,0:T(8,128)S(1)}, f32[1024,256]{1,0:T(8,128)S(1)}, u32[]{:S(2)}, u32[]{:S(2)}) collective-permute-start(f32[1024,256]{1,0:T(8,128)S(1)} %collective-permute-done.6), channel_id=1, source_target_pairs={{0,4},{4,0},{8,12},{12,8},{16,20},{20,16},{24,28},{28,24},{1,5},{5... | collective-permute-start | bytes 3145736 | tf_op jit(solution)/shard_map/ppermute | solution.py:63
  213.7 2.0 collective-permute-start.5
  215.7 1.3 slice_dynamic-update-slice_fusion.14
  217.2 1.3 slice_dynamic-update-slice_fusion.12
  219.2 2.6 fusion.44
  221.8 1.9 fusion.45
  223.7 6.6 %reshape.59 = f32[1024,4,2,128]{3,2,1,0:T(2,128)} reshape(f32[1024,1024]{1,0:T(8,128)} %all-gather.3.cloned.1.call-done) | data formatting | bytes 8388608 | tf_op jit(solution)/shard_map/reshape | solution.py:76
  230.3 15.1 %slice_reduce_fusion.1 = (f32[1024,4,128]{2,1,0:T(4,128)S(1)}, f32[1024,4,128]{2,1,0:T(4,128)S(1)}) fusion(f32[1024,4,2,128]{3,2,1,0:T(2,128)} %reshape.59), kind=kLoop, calls=%fused_computation.39 | loop fusion | bytes 8388608 | tf_op jit(solution)/shard_map/slice | solution.py:79
  245.5 7.1 %fusion.8 = f32[1024,2048]{1,0:T(8,128)S(1)} fusion(f32[1024,512]{1,0:T(8,128)S(1)} %copy-done.2, f32[1024,512]{1,0:T(8,128)S(1)} %get-tuple-element.13, f32[128,8,4,128]{3,2,1,0:T(4,128)S(1)} %bitcast.53), kind=kOutput, calls=%fused_computation.28 | convolution fusion | flops 6443499520 | bytes 14680064 | tf_op jit(solution)/shard_map/dot_general | solution.py:8
  252.6 12.1 %add_multiply_fusion = f32[1024,2048]{1,0:T(8,128)} fusion(f32[1024,2048]{1,0:T(8,128)} %param.6, f32[1024,2048]{1,0:T(8,128)S(1)} %fusion.8, f32[1024,512]{1,0:T(8,128)S(1)} %copy-done.4, f32[1024,512]{1,0:T(8,128)S(1)} %copy-done.3, f32[128,8,4,128]{3,2,1,0:T(4,128)S(1)} %bitcast.54), kind=kOutput, calls=%fused_computation.5 | convolution fusion | flops 6447693824 | bytes 31457280 | tf_op jit(solution)/shard_map/dot_general | solution.py:8
  264.7 10.9 %fusion.9 = f32[1024,512]{1,0:T(8,128)} fusion(f32[1024,2048]{1,0:T(8,128)} %add_multiply_fusion, f32[1024,512]{1,0:T(8,128)S(1)} %copy-done.4, f32[1024,512]{1,0:T(8,128)S(1)} %copy-done.3), kind=kOutput, calls=%fused_computation.29 | convolution fusion | flops 6443499520 | bytes 14680064 | tf_op jit(solution)/shard_map/dot_general | solution.py:8
  275.7 10.9 %fusion.7 = f32[1024,512]{1,0:T(8,128)} fusion(f32[1024,2048]{1,0:T(8,128)} %add_multiply_fusion, f32[1024,512]{1,0:T(8,128)} %get-tuple-element.14, f32[1024,512]{1,0:T(8,128)S(1)} %get-tuple-element.13), kind=kOutput, calls=%fused_computation.27 | convolution fusion | flops 6443499520 | bytes 14680064 | tf_op jit(solution)/shard_map/dot_general | solution.py:8
  286.7 49.9 %reduce-scatter.5.cloned.1.call-done = f32[1024,128]{1,0:T(8,128)} async-done(((f32[1024,512]{1,0:T(8,128)}), f32[1024,128]{1,0:T(8,128)}) %reduce-scatter.5.cloned.1.call-update) | async-done | bytes 524304 | tf_op jit(solution)/shard_map/reduce_scatter | solution.py:86
  336.6 1.7 collective-permute-start.8
  338.3 54.2 %collective-permute-start.10 = (f32[1024,128]{1,0:T(8,128)S(1)}, f32[1024,128]{1,0:T(8,128)S(1)}, u32[]{:S(2)}, u32[]{:S(2)}) collective-permute-start(f32[1024,128]{1,0:T(8,128)S(1)} %collective-permute-done.8), channel_id=1, source_target_pairs={{0,8},{4,12},{8,0},{12,4},{16,24},{20,28},{24,16},{28,20},{1,9},{5... | collective-permute-start | bytes 1572872 | tf_op jit(solution)/shard_map/ppermute | solution.py:61
  392.5 1.7 collective-permute-start.14
  394.8 6.9 %collective-permute-start.9 = (f32[1024,128]{1,0:T(8,128)S(1)}, f32[1024,128]{1,0:T(8,128)}, u32[]{:S(2)}, u32[]{:S(2)}) collective-permute-start(f32[1024,128]{1,0:T(8,128)S(1)} %collective-permute-done.8), channel_id=1, source_target_pairs={{0,4},{4,0},{8,12},{12,8},{16,20},{20,16},{24,28},{28,24},{1,5},{5... | collective-permute-start | bytes 1572872 | tf_op jit(solution)/shard_map/ppermute | solution.py:63
  401.7 9.3 %collective-permute-start.11 = (f32[1024,128]{1,0:T(8,128)S(1)}, f32[1024,128]{1,0:T(8,128)S(1)}, u32[]{:S(2)}, u32[]{:S(2)}) collective-permute-start(f32[1024,128]{1,0:T(8,128)S(1)} %collective-permute-done.10), channel_id=1, source_target_pairs={{0,4},{4,0},{8,12},{12,8},{16,20},{20,16},{24,28},{28,24},{1,5},{5... | collective-permute-start | bytes 1572872 | tf_op jit(solution)/shard_map/ppermute | solution.py:63
  411.0 9.1 %reduce-precision_convert_fusion = bf16[2048,2048]{1,0:T(8,128)(2,1)} fusion(f32[2048,2048]{1,0:T(8,128)} %param.7), kind=kLoop, calls=%fused_computation.2 | loop fusion | flops 8388608 | bytes 25165824 | tf_op jit(solution)/shard_map/convert_element_type | solution.py:19
  420.2 1.7 collective-permute-start.16
  421.9 2.7 collective-permute-start.13
  427.7 8.7 %fusion.12 = f32[2048,512]{1,0:T(8,128)S(1)} fusion(f32[2048,2048]{1,0:T(8,128)} %param.7, f32[1024,512]{1,0:T(8,128)S(1)} %get-tuple-element.8, f32[1024,512]{1,0:T(8,128)S(1)} %get-tuple-element.7), kind=kOutput, calls=%fused_computation.31 | convolution fusion | flops 4310695936 | bytes 25165824 | tf_op jit(solution)/shard_map/dot_general | solution.py:23
  436.4 4.7 fusion.16
  441.1 6.9 %fusion.5 = f32[2048,512]{1,0:T(8,128)} fusion(f32[2048,512]{1,0:T(8,128)S(1)} %fusion.12, f32[512,2048]{0,1:T(8,128)S(1)} %fusion.16, bf16[2048,2048]{1,0:T(8,128)(2,1)S(1)} %bitcast.49, f32[1024,512]{1,0:T(8,128)S(1)} %get-tuple-element.8, f32[1024,512]{1,0:T(8,128)S(1)} %get-tuple-element.7), kind=kOutput, calls=%fused_computation.23 | convolution fusion | flops 4301258752 | bytes 25165824 | tf_op jit(solution)/shard_map/dot_general | solution.py:23
  448.1 3.5 collective-permute-start.18
  451.6 2.4 collective-permute-start.20
  454.0 1.4 collective-permute-start.22
  455.4 7.3 %collective-permute-start.17 = (f32[1024,128]{1,0:T(8,128)S(1)}, f32[1024,128]{1,0:T(8,128)S(1)}, u32[]{:S(2)}, u32[]{:S(2)}) collective-permute-start(f32[1024,128]{1,0:T(8,128)S(1)} %collective-permute-done.16), channel_id=1, source_target_pairs={{0,4},{4,0},{8,12},{12,8},{16,20},{20,16},{24,28},{28,24},{1,5},{5... | collective-permute-start | bytes 1572872 | tf_op jit(solution)/shard_map/ppermute | solution.py:63
  462.7 8.3 %collective-permute-start.19 = (f32[1024,128]{1,0:T(8,128)S(1)}, f32[1024,128]{1,0:T(8,128)S(1)}, u32[]{:S(2)}, u32[]{:S(2)}) collective-permute-start(f32[1024,128]{1,0:T(8,128)S(1)} %collective-permute-done.18), channel_id=1, source_target_pairs={{0,4},{4,0},{8,12},{12,8},{16,20},{20,16},{24,28},{28,24},{1,5},{5... | collective-permute-start | bytes 1572872 | tf_op jit(solution)/shard_map/ppermute | solution.py:63
  471.0 6.7 %collective-permute-done.20 = f32[1024,128]{1,0:T(8,128)S(1)} collective-permute-done((f32[1024,128]{1,0:T(8,128)S(1)}, f32[1024,128]{1,0:T(8,128)S(1)}, u32[]{:S(2)}, u32[]{:S(2)}) %collective-permute-start.20) | collective-permute-done | bytes 524320 | tf_op jit(solution)/shard_map/ppermute | solution.py:61
  477.7 2.0 collective-permute-start.21
  482.9 1.3 copy-done.5
  484.3 6.6 %fusion.14 = f32[512,2048]{0,1:T(8,128)} fusion(bf16[2048,2048]{1,0:T(8,128)(2,1)S(1)} %bitcast.51, f32[1024,512]{1,0:T(8,128)S(1)} %get-tuple-element.10, f32[1024,512]{1,0:T(8,128)S(1)} %get-tuple-element.9), kind=kOutput, calls=%fused_computation.32 | convolution fusion | flops 4299161600 | bytes 16777216 | tf_op jit(solution)/shard_map/dot_general | solution.py:23
  490.9 7.7 %fusion.10 = f32[2048,512]{1,0:T(8,128)} fusion(f32[2048,2048]{1,0:T(8,128)S(1)} %bitcast.47, f32[1024,512]{1,0:T(8,128)} %copy-done.5, f32[1024,512]{1,0:T(8,128)S(1)} %get-tuple-element.9), kind=kOutput, calls=%fused_computation.30 | convolution fusion | flops 4310695936 | bytes 25165824 | tf_op jit(solution)/shard_map/dot_general | solution.py:23
  498.6 13.2 %fusion.4 = f32[2048,512]{1,0:T(8,128)} fusion(f32[2048,512]{1,0:T(8,128)} %fusion.10, f32[512,2048]{0,1:T(8,128)} %fusion.14, bf16[2048,2048]{1,0:T(8,128)(2,1)} %reduce-precision_convert_fusion, f32[1024,512]{1,0:T(8,128)} %copy-done.5, f32[1024,512]{1,0:T(8,128)S(1)} %get-tuple-element.9), kind=kOutput, calls=%fused_computation.20 | convolution fusion | flops 4301258752 | bytes 25165824 | tf_op jit(solution)/shard_map/dot_general | solution.py:23
  511.9 22.5 %reduce-scatter.7.cloned.1.call-done = f32[2048,128]{1,0:T(8,128)} async-done(((f32[2048,512]{1,0:T(8,128)}), f32[2048,128]{1,0:T(8,128)}) %reduce-scatter.7.cloned.1.call-update) | async-done | bytes 1048592 | tf_op jit(solution)/shard_map/reduce_scatter | solution.py:89
  534.4 79.5 %reduce-scatter.11.cloned.1.call-done = f32[2048,128]{1,0:T(8,128)} async-done(((f32[2048,512]{1,0:T(8,128)}), f32[2048,128]{1,0:T(8,128)}) %reduce-scatter.11.cloned.1.call-update) | async-done | bytes 1048592 | tf_op jit(solution)/shard_map/reduce_scatter | solution.py:89
  613.9 3.0 pad_maximum_fusion.8
  (110 shorter events, 12.3 us)
Async XLA Ops:
  6.5 6.2 %copy-start = (f32[2048,256]{1,0:T(8,128)S(1)}, f32[2048,256]{1,0:T(8,128)}, u32[]{:S(2)}) copy-start(f32[2048,256]{1,0:T(8,128)} %param.4) | copy-start | bytes 6291460
  21.4 31.8 %all-to-all-start = ((f32[8,256,256]{2,1,0:T(8,128)}), f32[8,256,256]{2,1,0:T(8,128)S(1)}, u32[]{:S(2)}, u32[]{:S(2)}) async-start(f32[8,256,256]{2,1,0:T(8,128)} %bitcast.52), calls=%async_computation | async-start | bytes 4194304 | tf_op jit(solution)/shard_map/all_to_all | solution.py:55
  26.6 197.1 %all-gather.3.cloned.1.call-start = ((), (), s32[]{:S(2)}) async-start(), calls=%async_computation.9 | async-start | bytes 5242880 | tf_op jit(solution)/shard_map/all_gather | solution.py:75
  57.9 278.7 %reduce-scatter.5.cloned.1.call-start = ((), (), s32[]{:S(2)}) async-start(), calls=%async_computation.5 | async-start | bytes 2621440 | tf_op jit(solution)/shard_map/reduce_scatter | solution.py:86
  58.0 9.5 %collective-permute-start = (f32[1024,256]{1,0:T(8,128)}, f32[1024,256]{1,0:T(8,128)}, u32[]{:S(2)}, u32[]{:S(2)}) collective-permute-start(f32[1024,256]{1,0:T(8,128)} %gather_fusion.1), channel_id=1, source_target_pairs={{0,0},{1,4},{2,8},{3,12},{4,16},{5,20},{6,24},{7,28},{8,1},{9,5},{... | collective-permute-start | bytes 3145736 | tf_op jit(solution)/shard_map/ppermute | solution.py:59
  67.5 118.5 %collective-permute-start.2 = (f32[1024,256]{1,0:T(8,128)}, f32[1024,256]{1,0:T(8,128)S(1)}, u32[]{:S(2)}, u32[]{:S(2)}) collective-permute-start(f32[1024,256]{1,0:T(8,128)} %collective-permute-done), channel_id=1, source_target_pairs={{0,8},{4,12},{8,0},{12,4},{16,24},{20,28},{24,16},{28,20},{1,9},{5... | collective-permute-start | bytes 3145736 | tf_op jit(solution)/shard_map/ppermute | solution.py:61
  167.2 38.9 %collective-permute-start.6 = (f32[1024,256]{1,0:T(8,128)}, f32[1024,256]{1,0:T(8,128)S(1)}, u32[]{:S(2)}, u32[]{:S(2)}) collective-permute-start(f32[1024,256]{1,0:T(8,128)} %collective-permute-done), channel_id=1, source_target_pairs={{0,24},{4,28},{8,16},{12,20},{16,8},{20,12},{24,0},{28,4},{1,25},{... | collective-permute-start | bytes 3145736 | tf_op jit(solution)/shard_map/ppermute | solution.py:61
  167.2 46.5 %collective-permute-start.4 = (f32[1024,256]{1,0:T(8,128)}, f32[1024,256]{1,0:T(8,128)S(1)}, u32[]{:S(2)}, u32[]{:S(2)}) collective-permute-start(f32[1024,256]{1,0:T(8,128)} %collective-permute-done), channel_id=1, source_target_pairs={{0,16},{4,20},{8,24},{12,28},{16,0},{20,4},{24,8},{28,12},{1,17},{... | collective-permute-start | bytes 3145736 | tf_op jit(solution)/shard_map/ppermute | solution.py:61
  168.7 47.1 %collective-permute-start.1 = (f32[1024,256]{1,0:T(8,128)}, f32[1024,256]{1,0:T(8,128)}, u32[]{:S(2)}, u32[]{:S(2)}) collective-permute-start(f32[1024,256]{1,0:T(8,128)} %collective-permute-done), channel_id=1, source_target_pairs={{0,4},{4,0},{8,12},{12,8},{16,20},{20,16},{24,28},{28,24},{1,5},{5... | collective-permute-start | bytes 3145736 | tf_op jit(solution)/shard_map/ppermute | solution.py:63
  186.0 31.2 %collective-permute-start.3 = (f32[1024,256]{1,0:T(8,128)S(1)}, f32[1024,256]{1,0:T(8,128)}, u32[]{:S(2)}, u32[]{:S(2)}) collective-permute-start(f32[1024,256]{1,0:T(8,128)S(1)} %collective-permute-done.2), channel_id=1, source_target_pairs={{0,4},{4,0},{8,12},{12,8},{16,20},{20,16},{24,28},{28,24},{1,5},{5... | collective-permute-start | bytes 3145736 | tf_op jit(solution)/shard_map/ppermute | solution.py:63
  206.1 13.0 %collective-permute-start.7 = (f32[1024,256]{1,0:T(8,128)S(1)}, f32[1024,256]{1,0:T(8,128)S(1)}, u32[]{:S(2)}, u32[]{:S(2)}) collective-permute-start(f32[1024,256]{1,0:T(8,128)S(1)} %collective-permute-done.6), channel_id=1, source_target_pairs={{0,4},{4,0},{8,12},{12,8},{16,20},{20,16},{24,28},{28,24},{1,5},{5... | collective-permute-start | bytes 3145736 | tf_op jit(solution)/shard_map/ppermute | solution.py:63
  213.7 5.0 collective-permute-start.5
  230.3 15.1 %copy-start.2 = (f32[1024,512]{1,0:T(8,128)S(1)}, f32[1024,512]{1,0:T(8,128)}, u32[]{:S(2)}) copy-start(f32[1024,512]{1,0:T(8,128)} %get-tuple-element.14) | copy-start | bytes 6291460
  245.5 7.1 %copy-start.3 = (f32[1024,512]{1,0:T(8,128)S(1)}, f32[1024,512]{1,0:T(8,128)}, u32[]{:S(2)}) copy-start(f32[1024,512]{1,0:T(8,128)} %get-tuple-element.11) | copy-start | bytes 6291460
  245.5 7.1 %copy-start.4 = (f32[1024,512]{1,0:T(8,128)S(1)}, f32[1024,512]{1,0:T(8,128)}, u32[]{:S(2)}) copy-start(f32[1024,512]{1,0:T(8,128)} %get-tuple-element.12) | copy-start | bytes 6291460
  275.6 144.5 %reduce-scatter.9.cloned.1.call-start = ((), (), s32[]{:S(2)}) async-start(), calls=%async_computation.7 | async-start | bytes 2621440 | tf_op jit(solution)/shard_map/reduce_scatter | solution.py:86
  286.6 247.7 %reduce-scatter.7.cloned.1.call-start = ((), (), s32[]{:S(2)}) async-start(), calls=%async_computation.6 | async-start | bytes 5242880 | tf_op jit(solution)/shard_map/reduce_scatter | solution.py:89
  336.6 1.7 collective-permute-start.8
  338.3 63.4 %collective-permute-start.10 = (f32[1024,128]{1,0:T(8,128)S(1)}, f32[1024,128]{1,0:T(8,128)S(1)}, u32[]{:S(2)}, u32[]{:S(2)}) collective-permute-start(f32[1024,128]{1,0:T(8,128)S(1)} %collective-permute-done.8), channel_id=1, source_target_pairs={{0,8},{4,12},{8,0},{12,4},{16,24},{20,28},{24,16},{28,20},{1,9},{5... | collective-permute-start | bytes 1572872 | tf_op jit(solution)/shard_map/ppermute | solution.py:61
  392.5 32.7 %collective-permute-start.14 = (f32[1024,128]{1,0:T(8,128)S(1)}, f32[1024,128]{1,0:T(8,128)S(1)}, u32[]{:S(2)}, u32[]{:S(2)}) collective-permute-start(f32[1024,128]{1,0:T(8,128)S(1)} %collective-permute-done.8), channel_id=1, source_target_pairs={{0,24},{4,28},{8,16},{12,20},{16,8},{20,12},{24,0},{28,4},{1,25},{... | collective-permute-start | bytes 1572872 | tf_op jit(solution)/shard_map/ppermute | solution.py:61
  394.2 27.6 %collective-permute-start.12 = (f32[1024,128]{1,0:T(8,128)S(1)}, f32[1024,128]{1,0:T(8,128)S(1)}, u32[]{:S(2)}, u32[]{:S(2)}) collective-permute-start(f32[1024,128]{1,0:T(8,128)S(1)} %collective-permute-done.8), channel_id=1, source_target_pairs={{0,16},{4,20},{8,24},{12,28},{16,0},{20,4},{24,8},{28,12},{1,17},{... | collective-permute-start | bytes 1572872 | tf_op jit(solution)/shard_map/ppermute | solution.py:61
  394.8 30.5 %collective-permute-start.9 = (f32[1024,128]{1,0:T(8,128)S(1)}, f32[1024,128]{1,0:T(8,128)}, u32[]{:S(2)}, u32[]{:S(2)}) collective-permute-start(f32[1024,128]{1,0:T(8,128)S(1)} %collective-permute-done.8), channel_id=1, source_target_pairs={{0,4},{4,0},{8,12},{12,8},{16,20},{20,16},{24,28},{28,24},{1,5},{5... | collective-permute-start | bytes 1572872 | tf_op jit(solution)/shard_map/ppermute | solution.py:63
  401.7 24.7 %collective-permute-start.11 = (f32[1024,128]{1,0:T(8,128)S(1)}, f32[1024,128]{1,0:T(8,128)S(1)}, u32[]{:S(2)}, u32[]{:S(2)}) collective-permute-start(f32[1024,128]{1,0:T(8,128)S(1)} %collective-permute-done.10), channel_id=1, source_target_pairs={{0,4},{4,0},{8,12},{12,8},{16,20},{20,16},{24,28},{28,24},{1,5},{5... | collective-permute-start | bytes 1572872 | tf_op jit(solution)/shard_map/ppermute | solution.py:63
  420.2 27.9 %collective-permute-start.16 = (f32[1024,128]{1,0:T(8,128)}, f32[1024,128]{1,0:T(8,128)S(1)}, u32[]{:S(2)}, u32[]{:S(2)}) collective-permute-start(f32[1024,128]{1,0:T(8,128)} %reduce-scatter.9.cloned.1.call-done), channel_id=1, source_target_pairs={{0,0},{1,4},{2,8},{3,12},{4,16},{5,20},{6,24},{7,28},{8,1},{9,5},{... | collective-permute-start | bytes 1572872 | tf_op jit(solution)/shard_map/ppermute | solution.py:59
  421.9 4.7 collective-permute-start.13
  425.2 2.0 collective-permute-start.15
  427.2 9.2 %slice-start.4 = ((s8[8388608]{0:T(1024)(128)(4,1)}), s8[4194304]{0:T(1024)(128)(4,1)S(1)}, s32[]{:S(2)}) async-start(s8[8388608]{0:T(1024)(128)(4,1)} %bitcast.48), calls=%async_computation.14 | async-start | bytes 8388608
  427.7 8.7 %slice-start.5 = ((s8[8388608]{0:T(1024)(128)(4,1)}), s8[4194304]{0:T(1024)(128)(4,1)S(1)}, s32[]{:S(2)}) async-start(s8[8388608]{0:T(1024)(128)(4,1)} %bitcast.48), calls=%async_computation.15 | async-start | bytes 8388608
  448.0 165.8 %reduce-scatter.11.cloned.1.call-start = ((), (), s32[]{:S(2)}) async-start(), calls=%async_computation.8 | async-start | bytes 5242880 | tf_op jit(solution)/shard_map/reduce_scatter | solution.py:89
  448.1 14.6 %collective-permute-start.18 = (f32[1024,128]{1,0:T(8,128)S(1)}, f32[1024,128]{1,0:T(8,128)S(1)}, u32[]{:S(2)}, u32[]{:S(2)}) collective-permute-start(f32[1024,128]{1,0:T(8,128)S(1)} %collective-permute-done.16), channel_id=1, source_target_pairs={{0,8},{4,12},{8,0},{12,4},{16,24},{20,28},{24,16},{28,20},{1,9},{5... | collective-permute-start | bytes 1572872 | tf_op jit(solution)/shard_map/ppermute | solution.py:61
  451.6 26.1 %collective-permute-start.20 = (f32[1024,128]{1,0:T(8,128)S(1)}, f32[1024,128]{1,0:T(8,128)S(1)}, u32[]{:S(2)}, u32[]{:S(2)}) collective-permute-start(f32[1024,128]{1,0:T(8,128)S(1)} %collective-permute-done.16), channel_id=1, source_target_pairs={{0,16},{4,20},{8,24},{12,28},{16,0},{20,4},{24,8},{28,12},{1,17},{... | collective-permute-start | bytes 1572872 | tf_op jit(solution)/shard_map/ppermute | solution.py:61
  454.0 26.3 %collective-permute-start.22 = (f32[1024,128]{1,0:T(8,128)S(1)}, f32[1024,128]{1,0:T(8,128)S(1)}, u32[]{:S(2)}, u32[]{:S(2)}) collective-permute-start(f32[1024,128]{1,0:T(8,128)S(1)} %collective-permute-done.16), channel_id=1, source_target_pairs={{0,24},{4,28},{8,16},{12,20},{16,8},{20,12},{24,0},{28,4},{1,25},{... | collective-permute-start | bytes 1572872 | tf_op jit(solution)/shard_map/ppermute | solution.py:61
  455.4 25.0 %collective-permute-start.17 = (f32[1024,128]{1,0:T(8,128)S(1)}, f32[1024,128]{1,0:T(8,128)S(1)}, u32[]{:S(2)}, u32[]{:S(2)}) collective-permute-start(f32[1024,128]{1,0:T(8,128)S(1)} %collective-permute-done.16), channel_id=1, source_target_pairs={{0,4},{4,0},{8,12},{12,8},{16,20},{20,16},{24,28},{28,24},{1,5},{5... | collective-permute-start | bytes 1572872 | tf_op jit(solution)/shard_map/ppermute | solution.py:63
  462.7 17.9 %collective-permute-start.19 = (f32[1024,128]{1,0:T(8,128)S(1)}, f32[1024,128]{1,0:T(8,128)S(1)}, u32[]{:S(2)}, u32[]{:S(2)}) collective-permute-start(f32[1024,128]{1,0:T(8,128)S(1)} %collective-permute-done.18), channel_id=1, source_target_pairs={{0,4},{4,0},{8,12},{12,8},{16,20},{20,16},{24,28},{28,24},{1,5},{5... | collective-permute-start | bytes 1572872 | tf_op jit(solution)/shard_map/ppermute | solution.py:63
  477.7 3.6 collective-permute-start.21
  480.3 4.0 slice-start.6
  480.4 2.0 collective-permute-start.23
  481.4 2.8 slice-start.7
  482.4 8.4 %slice-start = ((s8[16777216]{0:T(1024)(128)(4,1)}), s8[4194304]{0:T(1024)(128)(4,1)S(1)}, s32[]{:S(2)}) async-start(s8[16777216]{0:T(1024)(128)(4,1)} %bitcast.46), calls=%async_computation.10 | async-start | bytes 8388608
  482.9 1.3 copy-start.5
  484.2 6.6 %slice-start.1 = ((s8[16777216]{0:T(1024)(128)(4,1)}), s8[4194304]{0:T(1024)(128)(4,1)S(1)}, s32[]{:S(2)}) async-start(s8[16777216]{0:T(1024)(128)(4,1)} %bitcast.46), calls=%async_computation.11 | async-start | bytes 8388608
  484.2 6.6 %slice-start.2 = ((s8[16777216]{0:T(1024)(128)(4,1)}), s8[4194304]{0:T(1024)(128)(4,1)S(1)}, s32[]{:S(2)}) async-start(s8[16777216]{0:T(1024)(128)(4,1)} %bitcast.46), calls=%async_computation.12 | async-start | bytes 8388608
  484.2 6.6 %slice-start.3 = ((s8[16777216]{0:T(1024)(128)(4,1)}), s8[4194304]{0:T(1024)(128)(4,1)S(1)}, s32[]{:S(2)}) async-start(s8[16777216]{0:T(1024)(128)(4,1)} %bitcast.46), calls=%async_computation.13 | async-start | bytes 8388608
  511.8 105.1 %copy-start.1 = (f32[2048,256]{1,0:T(8,128)S(1)}, f32[2048,256]{1,0:T(8,128)}, u32[]{:S(2)}) copy-start(f32[2048,256]{1,0:T(8,128)} %param.4) | copy-start | bytes 6291460
Sparse Core Ops, SparseCore 0:
  58.1 137.6 all-gather.2
  275.8 60.8 reduce-scatter.4
  339.0 70.9 reduce-scatter.8
  448.2 86.1 reduce-scatter.6
  536.6 77.2 reduce-scatter.10
